TPU v7x, 32 devices: a whole 2x2x4 slice. The times are simulated.
32 devices in a mesh: rows: 4 (over z), cols: 8 (over y, x, core).
Axes of the slice: x: 2, y: 2, z: 4, core: 2. Of those that a mesh axis runs over, the one named last changes fastest.
Arguments:
- slab: bfloat16 [8192, 8192], P('rows', 'cols'), may hold values from -6 to 6
- transforms: bfloat16 [8, 16384, 512], P('cols', 'rows'), may hold values from -0.25 to 0.25
- owners: int32 [2, 4], replicated, may hold values from 0 to 7, as said below
Outputs:
- updated: bfloat16 [8192, 8192], P('rows', 'cols')
Inputs may be any that keep to these rules, and one draw needn't show every extreme that they name: For each row block, the owners of different rounds differ.
All inputs are finite; a program needn't handle non-finite values.
Results may differ from a plain program's by a relative error of at most 0.0063.
Values may be sent and summed in bfloat16 or wider, within the bound.
No kernel may reach another device: no remote copies, remote signals or barrier semaphores. Data moves between devices by JAX's collectives and lax.ppermute only.
A program may use at most 64 MiB of HBM per device.

v0:
```python
import jax
import jax.numpy as jnp
from jax import lax
from jax.sharding import PartitionSpec as P


def spread(block, axis, owner):
    block = jnp.where(lax.axis_index(axis) == owner, block, jnp.zeros_like(block))
    return lax.psum(block, axis)


def shifted(value, axis, steps):
    count = lax.axis_size(axis)
    initial, last = (max(0, -steps), min(count, count - steps))
    return lax.ppermute(value, axis, [(source, source + steps) for source in range(initial, last)])


def apply_windows(transform_set, block_rows):
    product = jnp.einsum(
        "nab,nac->nbc", transform_set, block_rows, preferred_element_type=jnp.float32
    )
    return product.astype(jnp.bfloat16)


def local(slab, transforms, owners):
    row_block = lax.axis_index("rows")
    last_block = lax.axis_size("rows") - 1
    window = transforms.shape[2]
    own_slot = transforms[0]
    wins_count = own_slot.shape[0] // (2 * window)
    local_rows, local_cols = slab.shape
    border = window // 2
    matrix = slab
    for round_index in range(owners.shape[0]):
        owner = owners[round_index][row_block]
        received = spread(own_slot, "cols", owner).reshape(2, wins_count, window, window)
        matrix = apply_windows(received[0], matrix.reshape(wins_count, window, local_cols)).reshape(
            local_rows, local_cols
        )
        below = shifted(matrix[:border], "rows", -1)
        extended = jnp.concatenate([matrix[border:], below], 0).reshape(
            wins_count, window, local_cols
        )
        mixed = apply_windows(received[1], extended)
        final_window = jnp.where(
            row_block == last_block, extended[wins_count - 1], mixed[wins_count - 1]
        )
        mixed = jnp.concatenate([mixed[: wins_count - 1], final_window[None]], 0)
        flat = mixed.reshape(local_rows, local_cols)
        above, prev_transform = shifted(
            (matrix[local_rows - border :], received[1, wins_count - 1]), "rows", 1
        )
        crossing = jnp.concatenate([above, matrix[:border]], 0)
        top_new = lax.dot_general(
            prev_transform[:, border:],
            crossing,
            (((0,), (0,)), ((), ())),
            preferred_element_type=jnp.float32,
        )
        top_rows = jnp.where(row_block == 0, matrix[:border], top_new.astype(jnp.bfloat16))
        matrix = jnp.concatenate([top_rows, flat[: local_rows - border]], 0)
    return matrix


def solution(mesh):
    return jax.shard_map(
        local,
        mesh=mesh,
        in_specs=(P("rows", "cols"), P("cols", "rows", None), P()),
        out_specs=P("rows", "cols"),
        check_vma=False,
    )
```

profile of v0, /device:TPU:8, one launch (start us, length us, event | category | flops | bytes accessed | tf_op | source)
XLA Modules:
  0.0 218.1 jit_solution(13254833925161025590)
XLA Ops:
  6.5 0.8 fusion.22
  7.3 0.6 constant_dynamic-slice_fusion
  9.1 6.1 %select_bitcast_fusion = (bf16[4096,512]{1,0:T(8,128)(2,1)}, bf16[4096,512]{1,0:T(8,128)(2,1)}) fusion(bf16[1,4096,512]{2,1,0:T(8,128)(2,1)} %param.4, pred[]{:T(512)S(6)} %eq.16, pred[]{:T(512)S(6)} %eq.15), kind=kLoop, calls=%fused_computation.8 | loop fusion | flops 4194304 | bytes 12582914 | tf_op jit(solution)/shard_map/jit(_where)/select_n | solution.py:8
  15.2 128.2 %all-reduce.3.cloned.1.call-done = (bf16[4096,512]{1,0:T(8,128)(2,1)}, bf16[4096,512]{1,0:T(8,128)(2,1)}) async-done(((bf16[4096,512]{1,0:T(8,128)(2,1)}, bf16[4096,512]{1,0:T(8,128)(2,1)}), (bf16[4096,512]{1,0:T(8,128)(2,1)}, bf16[4096,512]{1,0:T(8,128)(2,1)})) %all-reduce.3.cloned.1.call-update) | async-done | bytes 8388624 | tf_op jit(solution)/shard_map/psum | solution.py:9
  143.4 2.7 %fusion.21 = (bf16[2048,512]{1,0:T(8,128)(2,1)S(1)}, bf16[2048,512]{1,0:T(8,128)(2,1)S(1)}) fusion(bf16[4096,512]{1,0:T(8,128)(2,1)} %get-tuple-element.6), kind=kLoop, calls=%fused_computation.43 | loop fusion | bytes 8388608 | tf_op jit(solution)/shard_map/slice | solution.py:44
  146.1 0.8 copy-done.1
  146.9 2.4 %convolution_convert_fusion.3 = bf16[4,512,1024]{2,1,0:T(8,128)(2,1)S(1)} fusion(bf16[4,512,512]{2,1,0:T(8,128)(2,1)S(1)} %bitcast.54, bf16[4,512,1024]{2,1,0:T(8,128)(2,1)S(1)} %bitcast.55), kind=kOutput, calls=%fused_computation.15 | convolution fusion | flops 2149580800 | bytes 10485760 | tf_op jit(solution)/shard_map/nab,nac->nbc/dot_general | solution.py:19
  149.8 1.3 slice_bitcast_fusion.1
  151.0 3.4 %collective-permute-start = (bf16[512,512]{1,0:T(8,128)(2,1)S(1)}, bf16[512,512]{1,0:T(8,128)(2,1)S(1)}, u32[]{:S(2)}, u32[]{:S(2)}) collective-permute-start(bf16[512,512]{1,0:T(8,128)(2,1)S(1)} %slice_bitcast_fusion.1), channel_id=1, source_target_pairs={{0,8},{8,16},{16,24},{1,9},{9,17},{17,25},{2,10},{10,18},{18,26},{... | collective-permute-start | bytes 1572872 | tf_op jit(solution)/shard_map/ppermute | solution.py:15
  154.4 3.4 %collective-permute-start.1 = (bf16[256,1024]{1,0:T(8,128)(2,1)S(1)}, bf16[256,1024]{1,0:T(8,128)(2,1)S(1)}, u32[]{:S(2)}, u32[]{:S(2)}) collective-permute-start(bf16[256,1024]{1,0:T(8,128)(2,1)S(1)} %get-tuple-element.11), channel_id=1, source_target_pairs={{0,8},{8,16},{16,24},{1,9},{9,17},{17,25},{2,10},{10,18},{18,26},{... | collective-permute-start | bytes 1572872 | tf_op jit(solution)/shard_map/ppermute | solution.py:15
  157.8 2.5 %collective-permute-start.2 = (bf16[256,1024]{1,0:T(8,128)(2,1)S(1)}, bf16[256,1024]{1,0:T(8,128)(2,1)S(1)}, u32[]{:S(2)}, u32[]{:S(2)}) collective-permute-start(bf16[256,1024]{1,0:T(8,128)(2,1)S(1)} %get-tuple-element.12), channel_id=1, source_target_pairs={{8,0},{16,8},{24,16},{9,1},{17,9},{25,17},{10,2},{18,10},{26,18},{... | collective-permute-start | bytes 1572872 | tf_op jit(solution)/shard_map/ppermute | solution.py:15
  160.6 11.7 %collective-permute-done.2 = bf16[256,1024]{1,0:T(8,128)(2,1)S(1)} collective-permute-done((bf16[256,1024]{1,0:T(8,128)(2,1)S(1)}, bf16[256,1024]{1,0:T(8,128)(2,1)S(1)}, u32[]{:S(2)}, u32[]{:S(2)}) %collective-permute-start.2) | collective-permute-done | bytes 524320 | tf_op jit(solution)/shard_map/ppermute | solution.py:15
  172.8 2.4 %convolution_convert_fusion.2 = bf16[4,512,1024]{2,1,0:T(8,128)(2,1)S(1)} fusion(bf16[4,512,512]{2,1,0:T(8,128)(2,1)S(1)} %bitcast.53, bf16[4,512,1024]{2,1,0:T(8,128)(2,1)S(1)} %bitcast.49), kind=kOutput, calls=%fused_computation.14 | convolution fusion | flops 2149580800 | bytes 10485760 | tf_op jit(solution)/shard_map/nab,nac->nbc/dot_general | solution.py:19
  176.7 0.6 collective-permute-done.1
  177.3 0.5 fusion
  178.3 2.4 %convolution_convert_fusion.1 = bf16[4,512,1024]{2,1,0:T(8,128)(2,1)S(1)} fusion(bf16[4,512,512]{2,1,0:T(8,128)(2,1)S(1)} %bitcast.52, bf16[4,512,1024]{2,1,0:T(8,128)(2,1)S(1)} %bitcast.48), kind=kOutput, calls=%fused_computation.13 | convolution fusion | flops 2149580800 | bytes 10485760 | tf_op jit(solution)/shard_map/nab,nac->nbc/dot_general | solution.py:19
  180.8 2.1 collective-permute-start.5
  182.9 3.9 %collective-permute-start.3 = (bf16[512,512]{1,0:T(8,128)(2,1)S(1)}, bf16[512,512]{1,0:T(8,128)(2,1)S(1)}, u32[]{:S(2)}, u32[]{:S(2)}) collective-permute-start(bf16[512,512]{1,0:T(8,128)(2,1)S(1)} %slice_bitcast_fusion), channel_id=1, source_target_pairs={{0,8},{8,16},{16,24},{1,9},{9,17},{17,25},{2,10},{10,18},{18,26},{... | collective-permute-start | bytes 1572872 | tf_op jit(solution)/shard_map/ppermute | solution.py:15
  187.2 3.4 %collective-permute-start.4 = (bf16[256,1024]{1,0:T(8,128)(2,1)S(1)}, bf16[256,1024]{1,0:T(8,128)(2,1)S(1)}, u32[]{:S(2)}, u32[]{:S(2)}) collective-permute-start(bf16[256,1024]{1,0:T(8,128)(2,1)S(1)} %get-tuple-element.7), channel_id=1, source_target_pairs={{0,8},{8,16},{16,24},{1,9},{9,17},{17,25},{2,10},{10,18},{18,26},{... | collective-permute-start | bytes 1572872 | tf_op jit(solution)/shard_map/ppermute | solution.py:15
  190.7 4.2 %collective-permute-done.5 = bf16[256,1024]{1,0:T(8,128)(2,1)S(1)} collective-permute-done((bf16[256,1024]{1,0:T(8,128)(2,1)S(1)}, bf16[256,1024]{1,0:T(8,128)(2,1)S(1)}, u32[]{:S(2)}, u32[]{:S(2)}) %collective-permute-start.5) | collective-permute-done | bytes 524320 | tf_op jit(solution)/shard_map/ppermute | solution.py:15
  195.4 2.4 %convolution_convert_fusion = bf16[4,512,1024]{2,1,0:T(8,128)(2,1)S(1)} fusion(bf16[4,512,512]{2,1,0:T(8,128)(2,1)S(1)} %bitcast.51, bf16[4,512,1024]{2,1,0:T(8,128)(2,1)S(1)} %bitcast.50), kind=kOutput, calls=%fused_computation.12 | convolution fusion | flops 2149580800 | bytes 10485760 | tf_op jit(solution)/shard_map/nab,nac->nbc/dot_general | solution.py:19
  199.7 8.6 %collective-permute-done.4 = bf16[256,1024]{1,0:T(8,128)(2,1)S(1)} collective-permute-done((bf16[256,1024]{1,0:T(8,128)(2,1)S(1)}, bf16[256,1024]{1,0:T(8,128)(2,1)S(1)}, u32[]{:S(2)}, u32[]{:S(2)}) %collective-permute-start.4) | collective-permute-done | bytes 524320 | tf_op jit(solution)/shard_map/ppermute | solution.py:15
  208.3 0.5 fusion.1
  208.8 2.5 %pad_maximum_fusion.5 = bf16[2048,1024]{1,0:T(8,128)(2,1)} fusion(bf16[1792,1024]{1,0:T(8,128)(2,1)S(1)} %slice.129, bf16[256,1024]{1,0:T(8,128)(2,1)S(1)} %fusion.1), kind=kLoop, calls=%fused_computation.7 | loop fusion | flops 8388608 | bytes 8388608 | tf_op jit(solution)/shard_map/concatenate | solution.py:61
  (24 shorter events, 5.9 us)
Async XLA Ops:
  6.5 136.9 %all-reduce.3.cloned.1.call-start = ((), (), s32[]{:S(2)}) async-start(), calls=%async_computation | async-start | bytes 16777216 | tf_op jit(solution)/shard_map/psum | solution.py:9
  143.4 3.4 %copy-start.1 = (bf16[2048,1024]{1,0:T(8,128)(2,1)S(1)}, bf16[2048,1024]{1,0:T(8,128)(2,1)}, u32[]{:S(2)}) copy-start(bf16[2048,1024]{1,0:T(8,128)(2,1)} %param.3) | copy-start | bytes 12582916
  149.4 11.0 %copy-start = (bf16[4096,512]{1,0:T(8,128)(2,1)S(1)}, bf16[4096,512]{1,0:T(8,128)(2,1)}, u32[]{:S(2)}) copy-start(bf16[4096,512]{1,0:T(8,128)(2,1)} %get-tuple-element.5) | copy-start | bytes 12582916
  151.0 25.7 %collective-permute-start = (bf16[512,512]{1,0:T(8,128)(2,1)S(1)}, bf16[512,512]{1,0:T(8,128)(2,1)S(1)}, u32[]{:S(2)}, u32[]{:S(2)}) collective-permute-start(bf16[512,512]{1,0:T(8,128)(2,1)S(1)} %slice_bitcast_fusion.1), channel_id=1, source_target_pairs={{0,8},{8,16},{16,24},{1,9},{9,17},{17,25},{2,10},{10,18},{18,26},{... | collective-permute-start | bytes 1572872 | tf_op jit(solution)/shard_map/ppermute | solution.py:15
  154.4 22.9 %collective-permute-start.1 = (bf16[256,1024]{1,0:T(8,128)(2,1)S(1)}, bf16[256,1024]{1,0:T(8,128)(2,1)S(1)}, u32[]{:S(2)}, u32[]{:S(2)}) collective-permute-start(bf16[256,1024]{1,0:T(8,128)(2,1)S(1)} %get-tuple-element.11), channel_id=1, source_target_pairs={{0,8},{8,16},{16,24},{1,9},{9,17},{17,25},{2,10},{10,18},{18,26},{... | collective-permute-start | bytes 1572872 | tf_op jit(solution)/shard_map/ppermute | solution.py:15
  157.8 14.5 %collective-permute-start.2 = (bf16[256,1024]{1,0:T(8,128)(2,1)S(1)}, bf16[256,1024]{1,0:T(8,128)(2,1)S(1)}, u32[]{:S(2)}, u32[]{:S(2)}) collective-permute-start(bf16[256,1024]{1,0:T(8,128)(2,1)S(1)} %get-tuple-element.12), channel_id=1, source_target_pairs={{8,0},{16,8},{24,16},{9,1},{17,9},{25,17},{10,2},{18,10},{26,18},{... | collective-permute-start | bytes 1572872 | tf_op jit(solution)/shard_map/ppermute | solution.py:15
  180.8 14.1 %collective-permute-start.5 = (bf16[256,1024]{1,0:T(8,128)(2,1)S(1)}, bf16[256,1024]{1,0:T(8,128)(2,1)S(1)}, u32[]{:S(2)}, u32[]{:S(2)}) collective-permute-start(bf16[256,1024]{1,0:T(8,128)(2,1)S(1)} %get-tuple-element.8), channel_id=1, source_target_pairs={{8,0},{16,8},{24,16},{9,1},{17,9},{25,17},{10,2},{18,10},{26,18},{... | collective-permute-start | bytes 1572872 | tf_op jit(solution)/shard_map/ppermute | solution.py:15
  182.9 16.8 %collective-permute-start.3 = (bf16[512,512]{1,0:T(8,128)(2,1)S(1)}, bf16[512,512]{1,0:T(8,128)(2,1)S(1)}, u32[]{:S(2)}, u32[]{:S(2)}) collective-permute-start(bf16[512,512]{1,0:T(8,128)(2,1)S(1)} %slice_bitcast_fusion), channel_id=1, source_target_pairs={{0,8},{8,16},{16,24},{1,9},{9,17},{17,25},{2,10},{10,18},{18,26},{... | collective-permute-start | bytes 1572872 | tf_op jit(solution)/shard_map/ppermute | solution.py:15
  187.2 21.1 %collective-permute-start.4 = (bf16[256,1024]{1,0:T(8,128)(2,1)S(1)}, bf16[256,1024]{1,0:T(8,128)(2,1)S(1)}, u32[]{:S(2)}, u32[]{:S(2)}) collective-permute-start(bf16[256,1024]{1,0:T(8,128)(2,1)S(1)} %get-tuple-element.7), channel_id=1, source_target_pairs={{0,8},{8,16},{16,24},{1,9},{9,17},{17,25},{2,10},{10,18},{18,26},{... | collective-permute-start | bytes 1572872 | tf_op jit(solution)/shard_map/ppermute | solution.py:15
Sparse Core Ops, SparseCore 0:
  15.3 128.0 all-reduce.2
where the time goes:
time: 219 us; the launch traced here: 218 us
  waiting for transfers between devices  154 us (70%)
  starting transfers between devices  18.7 us (9%)
  between operations  14.9 us (7%)
  other arithmetic  11.4 us (5%)
  matrix products  10.6 us (5%)
  local copies, waits for them, and re-layouts  8.63 us (4%)
    psum x1, waiting for transfers between devices, spread(): return lax.psum(block, axis)  128 us
    ppermute x6, waiting for transfers between devices, shifted(): lax.ppermute(value, axis, [(source, source + steps) for source in range(i...  25.5 us
    ppermute x6, starting transfers between devices, shifted(): lax.ppermute(value, axis, [(source, source + steps) for source in range(i...  18.7 us
    dot_general x4, matrix products, apply_windows(): jnp.einsum('nab,nac->nbc', transform_set, block_rows, preferred_element_t...  9.73 us
    select_n x1, other arithmetic, spread(): jnp.where(lax.axis_index(axis) == owner, block, jnp.zeros_like(block))  6.08 us
  transfers between devices with their start and end apart: 7, of which 6 were waited for; matrix products, arithmetic and copies ran while one was open for 4% of the time, Pallas kernels for 0%

commit v1 on v0

v1 whole, which is shorter than its diff:
```python
import jax
import jax.numpy as jnp
from jax import lax
from jax.experimental import pallas as pl
from jax.experimental.pallas import tpu as pltpu
from jax.sharding import PartitionSpec as P


def shifted(value, axis, steps):
    count = lax.axis_size(axis)
    initial, last = (max(0, -steps), min(count, count - steps))
    return lax.ppermute(value, axis, [(source, source + steps) for source in range(initial, last)])


def copy_all(copies):
    for copy in copies:
        copy.start()
    for copy in copies:
        copy.wait()


def small(flops=0, bytes_accessed=0):
    return dict(
        compiler_params=pltpu.CompilerParams(vmem_limit_bytes=1 << 20),
        cost_estimate=pl.CostEstimate(
            flops=flops, bytes_accessed=bytes_accessed, transcendentals=0
        ),
    )


ANY = pl.BlockSpec(memory_space=pl.ANY)


def runs(ms):
    found = []
    for at, m in enumerate(ms):
        if found and found[-1][0] + found[-1][2] == m:
            found[-1][2] += 1
        else:
            found.append([m, at, 1])
    return found


def take_half(order, own, slot):
    _, _, rows, width = slot.shape
    spans = runs(order)

    def kernel(source, out, sems):
        core = lax.axis_index("cols") & 1
        half = core if own else 1 - core
        copy_all(
            [
                pltpu.make_async_copy(source.at[pl.ds(first, n), half], out.at[pl.ds(at, n)], sems.at[k])
                for k, (first, at, n) in enumerate(spans)
            ]
        )

    return pl.pallas_call(
        kernel,
        out_shape=jax.ShapeDtypeStruct((len(order), rows, width), slot.dtype),
        in_specs=[ANY],
        out_specs=ANY,
        scratch_shapes=[pltpu.SemaphoreType.DMA((len(spans),))],
        name="take_half",
        **small(bytes_accessed=2 * slot.size),
    )(slot)


def place(half, other):
    n, rows, width = half.shape

    def kernel(mine, theirs, out, sems):
        core = lax.axis_index("cols") & 1
        copy_all(
            [
                pltpu.make_async_copy(
                    piece, out.at[:, pl.ds(pl.multiple_of(at * rows, rows), rows), :], sems.at[k]
                )
                for k, (piece, at) in enumerate(((mine, core), (theirs, 1 - core)))
            ]
        )

    return pl.pallas_call(
        kernel,
        out_shape=jax.ShapeDtypeStruct((n, 2 * rows, width), half.dtype),
        in_specs=[ANY] * 2,
        out_specs=ANY,
        scratch_shapes=[pltpu.SemaphoreType.DMA((2,))],
        name="place",
        **small(bytes_accessed=8 * n * rows * width),
    )(half, other)


def swap_cores(value):
    count = lax.axis_size("cols")
    return lax.ppermute(value, "cols", [(d, d ^ 1) for d in range(count)])


class Spread:
    def __init__(self, slot, owners_here, groups):
        count = lax.axis_size("cols")
        self.me = lax.axis_index("cols")
        self.core = self.me & 1
        self.owners = owners_here
        order = [m for group in groups for m in group]
        self.spans, at = [], 0
        for group in groups:
            self.spans.append(slice(at, at + len(group)))
            at += len(group)
        self.theirs = swap_cores(take_half(order, False, slot))
        self.own = take_half(order, True, slot)
        chips = [k ^ (k >> 1) for k in range(count // 2)]
        self.rings = [[2 * chip + core for chip in chips] for core in range(2)]
        self.sums = 0

    def sum(self, round_index, group):
        owner = self.owners[round_index]
        span = self.spans[group]
        value = jnp.where((owner & 1) == self.core, self.own[span], self.theirs[span])
        value = jnp.where((owner >> 1) == (self.me >> 1), value, jnp.zeros_like(value))
        turn = self.sums % len(self.rings[0])
        self.sums += 1
        return lax.psum(value, "cols", axis_index_groups=[ring[turn:] + ring[:turn] for ring in self.rings])

    def join(self, half):
        return place(half, swap_cores(half))

    def join_above(self, half):
        both = shifted(half, "rows", 1)
        return place(both[None], swap_cores(both)[None])[0]


def apply(q, x):
    product = lax.dot_general(q, x, (((0,), (0,)), ((), ())), preferred_element_type=jnp.float32)
    return product.astype(jnp.bfloat16)


def apply_many(q, x):
    product = jnp.einsum("nab,nac->nbc", q, x, preferred_element_type=jnp.float32)
    return product.astype(jnp.bfloat16)


def local(slab, transforms, owners):
    row_block = lax.axis_index("rows")
    last_block = lax.axis_size("rows") - 1
    window = transforms.shape[2]
    border = window // 2
    local_rows, local_cols = slab.shape
    wins = local_rows // window
    rounds = owners.shape[0]
    slot = transforms[0].reshape(2 * wins, 2, border, window)
    edge = [0, wins - 1, 2 * wins - 1]
    inside = [m for m in range(2 * wins) if m not in edge]
    spread = Spread(slot, owners[:, row_block], (edge, inside))

    halves = [[spread.sum(r, g) for g in range(2)] for r in range(rounds)]

    matrix = slab
    for r in range(rounds):
        head, tail = halves[r]
        edges = spread.join(head)
        head_rows = apply(edges[0], matrix[:window])
        tail_rows = apply(edges[1], matrix[local_rows - window :])
        begin, end = head_rows[:border], tail_rows[border:]
        below = shifted(begin, "rows", -1)
        above = shifted(end, "rows", 1)
        prev = spread.join_above(head[-1, :, border:])
        rest = spread.join(tail)
        mid = apply_many(
            rest[: wins - 2],
            matrix[window : local_rows - window].reshape(wins - 2, window, local_cols),
        ).reshape(local_rows - 2 * window, local_cols)
        centre = jnp.concatenate([head_rows[border:], mid, tail_rows[:border]], 0)
        inner = apply_many(rest[wins - 2 :], centre.reshape(wins - 1, window, local_cols)).reshape(
            local_rows - window, local_cols
        )
        low = apply(edges[2, :, :border], jnp.concatenate([end, below], 0))
        low = jnp.where(row_block == last_block, end, low)
        top = apply(prev, jnp.concatenate([above, begin], 0))
        top = jnp.where(row_block == 0, begin, top)
        matrix = jnp.concatenate([top, inner, low], 0)
    return matrix


def solution(mesh):
    return jax.shard_map(
        local,
        mesh=mesh,
        in_specs=(P("rows", "cols"), P("cols", "rows", None), P()),
        out_specs=P("rows", "cols"),
        check_vma=False,
    )
```

time: 219 us -> 285 us (1.30)
  waiting for transfers between devices: 154 us -> 203 us
  local copies, waits for them, and re-layouts: 8.63 us -> 15 us
  matrix products: 10.6 us -> 16.3 us
  Pallas kernels: 0 us -> 4.95 us
  other arithmetic: 11.4 us -> 8.47 us
    psum x1 -> x4, waiting for transfers between devices: 128 us -> 190 us  [sum(): lax.psum(value, 'cols', axis_index_groups=[ring[turn:] + ring[:turn] for...]
    ppermute x6, waiting for transfers between devices: 25.5 us -> 9.02 us  [shifted(): lax.ppermute(value, axis, [(source, source + steps) for source in range(i...]
    unnamed x4 -> x26, local copies, waits for them, and re-layouts: 0.79 us -> 8.71 us
    dot_general x6 -> x12, matrix products: 10.6 us -> 16.3 us  [the longest x8 8.97 us: apply(): lax.dot_general(q, x, (((0,), (0,)), ((), ())), preferred_element_type=jn...]
    pallas_call x0 -> x8, Pallas kernels: none -> 4.95 us  [the longest x6 3.33 us: place(): pl.pallas_call(kernel, out_shape=jax.ShapeDtypeStruct((n, 2 * rows, width...]
    slice x11 -> x8, local copies, waits for them, and re-layouts: 5.95 us -> 4.4 us  [the longest x4 2.27 us: local(): centre = jnp.concatenate([head_rows[border:], mid, tail_rows[:border]], 0)]
    select_n x3 -> x2, other arithmetic: 6.94 us -> 5.42 us  [sum(): value = jnp.where(owner >> 1 == self.me >> 1, value, jnp.zeros_like(value))]
  transfers between devices with their start and end apart: 7 -> 17, of which waited for: 6 -> 7; matrix products, arithmetic and copies ran while one was open for 4% -> 9% of each run, Pallas kernels for 0% -> 1%
where the time goes in v1:
time: 285 us; the launch traced here: 283 us
  waiting for transfers between devices  203 us (71%)
  starting transfers between devices  19.3 us (7%)
  matrix products  16.3 us (6%)
  between operations  16.3 us (6%)
  local copies, waits for them, and re-layouts  15 us (5%)
  other arithmetic  8.47 us (3%)
  Pallas kernels  4.95 us (2%)
    psum x4, waiting for transfers between devices, sum(): lax.psum(value, 'cols', axis_index_groups=[ring[turn:] + ring[:turn] for...  190 us
    ppermute x6, starting transfers between devices, shifted(): lax.ppermute(value, axis, [(source, source + steps) for source in range(i...  18.8 us
    ppermute x6, waiting for transfers between devices, shifted(): lax.ppermute(value, axis, [(source, source + steps) for source in range(i...  9.02 us
    dot_general x8, matrix products, apply(): lax.dot_general(q, x, (((0,), (0,)), ((), ())), preferred_element_type=jn...  8.97 us
    unnamed x26, local copies, waits for them, and re-layouts  8.71 us
    dot_general x4, matrix products, apply_many(): jnp.einsum('nab,nac->nbc', q, x, preferred_element_type=jnp.float32)  7.28 us
  transfers between devices with their start and end apart: 17, of which 7 were waited for; matrix products, arithmetic and copies ran while one was open for 9% of the time, Pallas kernels for 1%

profile of v1, /device:TPU:8, one launch (start us, length us, event | category | flops | bytes accessed | tf_op | source)
XLA Modules:
  0.0 282.9 jit_solution(17009415196380432497)
XLA Ops:
  6.5 2.2 copy-done.2
  8.7 1.4 take_half.3
  13.6 2.2 copy-done.3
  16.1 2.4 select_select_fusion.3
  19.3 3.0 %select_select_fusion = (bf16[5,256,512]{2,1,0:T(8,128)(2,1)}, bf16[5,256,512]{2,1,0:T(8,128)(2,1)}) fusion(pred[]{:T(512)S(6)} %eq.26, pred[]{:T(512)S(6)} %eq.25, bf16[8,256,512]{2,1,0:T(8,128)(2,1)} %collective-permute-done, bf16[8,256,512]{2,1,0:T(8,128)(2,1)S(1)} %take_half.2, pred[]{:T(512)S(6)} %eq.28, pred[]{:T(512)S(6)} %eq.27), kind=kLoop, calls=%fused_computation.11 | loop fusion | flops 2621440 | bytes 5242884 | tf_op jit(solution)/shard_map/jit(_where)/select_n | solution.py:120
  22.4 46.3 %all-reduce.7.cloned.1.call-done.mine = bf16[3,256,512]{2,1,0:T(8,128)(2,1)} async-done(((bf16[3,256,512]{2,1,0:T(8,128)(2,1)}), bf16[3,256,512]{2,1,0:T(8,128)(2,1)}) %all-reduce.7.cloned.1.call-update) | async-done | bytes 786448 | tf_op jit(solution)/shard_map/psum | solution.py:123
  68.8 52.1 %all-reduce.5.cloned.1.call-done.mine = bf16[3,256,512]{2,1,0:T(8,128)(2,1)} async-done(((bf16[3,256,512]{2,1,0:T(8,128)(2,1)}), bf16[3,256,512]{2,1,0:T(8,128)(2,1)}) %all-reduce.5.cloned.1.call-update) | async-done | bytes 786448 | tf_op jit(solution)/shard_map/psum | solution.py:123
  121.8 3.4 %collective-permute-start.7 = (bf16[256,256]{1,0:T(8,128)(2,1)S(1)}, bf16[256,256]{1,0:T(8,128)(2,1)S(1)}, u32[]{:S(2)}, u32[]{:S(2)}) collective-permute-start(bf16[256,256]{1,0:T(8,128)(2,1)S(1)} %slice_bitcast_fusion.12), channel_id=1, source_target_pairs={{0,8},{8,16},{16,24},{1,9},{9,17},{17,25},{2,10},{10,18},{18,26},{... | collective-permute-start | bytes 393224 | tf_op jit(solution)/shard_map/ppermute | solution.py:12
  126.1 3.4 %collective-permute-start.3 = (bf16[256,256]{1,0:T(8,128)(2,1)S(1)}, bf16[256,256]{1,0:T(8,128)(2,1)S(1)}, u32[]{:S(2)}, u32[]{:S(2)}) collective-permute-start(bf16[256,256]{1,0:T(8,128)(2,1)S(1)} %slice_bitcast_fusion.13), channel_id=1, source_target_pairs={{0,8},{8,16},{16,24},{1,9},{9,17},{17,25},{2,10},{10,18},{18,26},{... | collective-permute-start | bytes 393224 | tf_op jit(solution)/shard_map/ppermute | solution.py:12
  129.6 50.9 %all-reduce.9.cloned.1.call-done.mine = bf16[5,256,512]{2,1,0:T(8,128)(2,1)} async-done(((bf16[5,256,512]{2,1,0:T(8,128)(2,1)}), bf16[5,256,512]{2,1,0:T(8,128)(2,1)}) %all-reduce.9.cloned.1.call-update) | async-done | bytes 1310736 | tf_op jit(solution)/shard_map/psum | solution.py:123
  183.9 2.1 convolution_convert_fusion.7
  187.1 2.4 collective-permute-start.9
  191.4 3.4 %collective-permute-start.5 = (bf16[256,1024]{1,0:T(8,128)(2,1)}, bf16[256,1024]{1,0:T(8,128)(2,1)}, u32[]{:S(2)}, u32[]{:S(2)}) collective-permute-start(bf16[256,1024]{1,0:T(8,128)(2,1)} %get-tuple-element.16), channel_id=1, source_target_pairs={{0,8},{8,16},{16,24},{1,9},{9,17},{17,25},{2,10},{10,18},{18,26},{... | collective-permute-start | bytes 1572872 | tf_op jit(solution)/shard_map/ppermute | solution.py:12
  198.7 41.2 %all-reduce.11.cloned.1.call-done.mine = bf16[5,256,512]{2,1,0:T(8,128)(2,1)} async-done(((bf16[5,256,512]{2,1,0:T(8,128)(2,1)}), bf16[5,256,512]{2,1,0:T(8,128)(2,1)}) %all-reduce.11.cloned.1.call-update) | async-done | bytes 1310736 | tf_op jit(solution)/shard_map/psum | solution.py:123
  242.3 1.8 fusion.1
  244.2 1.9 fusion
  247.7 1.5 convolution_convert_fusion.3
  249.7 2.1 convolution_convert_fusion.1
  252.8 3.4 %collective-permute-start.10 = (bf16[256,1024]{1,0:T(8,128)(2,1)S(1)}, bf16[256,1024]{1,0:T(8,128)(2,1)S(1)}, u32[]{:S(2)}, u32[]{:S(2)}) collective-permute-start(bf16[256,1024]{1,0:T(8,128)(2,1)S(1)} %get-tuple-element.12), channel_id=1, source_target_pairs={{0,8},{8,16},{16,24},{1,9},{9,17},{17,25},{2,10},{10,18},{18,26},{... | collective-permute-start | bytes 1572872 | tf_op jit(solution)/shard_map/ppermute | solution.py:12
  257.0 2.8 collective-permute-start.12
  260.0 1.5 convolution_convert_fusion.2
  262.0 2.1 convolution_convert_fusion
  264.1 9.0 %collective-permute-done.12 = bf16[256,1024]{1,0:T(8,128)(2,1)S(1)} collective-permute-done((bf16[256,1024]{1,0:T(8,128)(2,1)S(1)}, bf16[256,1024]{1,0:T(8,128)(2,1)S(1)}, u32[]{:S(2)}, u32[]{:S(2)}) %collective-permute-start.12) | collective-permute-done | bytes 524320 | tf_op jit(solution)/shard_map/ppermute | solution.py:12
  274.1 2.3 pad_maximum_fusion
  (76 shorter events, 21.7 us)
Async XLA Ops:
  6.5 3.7 %copy-start = (s32[2,4]{1,0:T(2,128)S(1)}, s32[2,4]{1,0:T(2,128)}, u32[]{:S(2)}) copy-start(s32[2,4]{1,0:T(2,128)} %param.5) | copy-start | bytes 100
  6.5 62.2 %all-reduce.7.cloned.1.call-start = ((), (), s32[]{:S(2)}) async-start(), calls=%async_computation.1 | async-start | bytes 1572864 | tf_op jit(solution)/shard_map/psum | solution.py:123
  6.5 2.2 copy-start.2
  10.1 6.0 %collective-permute-start = (bf16[8,256,512]{2,1,0:T(8,128)(2,1)}, bf16[8,256,512]{2,1,0:T(8,128)(2,1)}, u32[]{:S(2)}, u32[]{:S(2)}) collective-permute-start(bf16[8,256,512]{2,1,0:T(8,128)(2,1)} %take_half.3), channel_id=1, source_target_pairs={{0,1},{1,0},{2,3},{3,2},{4,5},{5,4},{6,7},{7,6},{8,9},{9,8},{10,11... | collective-permute-start | bytes 6291464 | tf_op jit(solution)/shard_map/ppermute | solution.py:96
  13.6 2.2 copy-start.3
  18.5 102.3 %all-reduce.5.cloned.1.call-start = ((), (), s32[]{:S(2)}) async-start(), calls=%async_computation | async-start | bytes 1572864 | tf_op jit(solution)/shard_map/psum | solution.py:123
  19.3 161.2 %all-reduce.9.cloned.1.call-start = ((), (), s32[]{:S(2)}) async-start(), calls=%async_computation.2 | async-start | bytes 2621440 | tf_op jit(solution)/shard_map/psum | solution.py:123
  22.4 217.5 %all-reduce.11.cloned.1.call-start = ((), (), s32[]{:S(2)}) async-start(), calls=%async_computation.3 | async-start | bytes 2621440 | tf_op jit(solution)/shard_map/psum | solution.py:123
  68.7 111.7 %collective-permute-start.2 = (bf16[3,256,512]{2,1,0:T(8,128)(2,1)}, bf16[3,256,512]{2,1,0:T(8,128)(2,1)S(1)}, u32[]{:S(2)}, u32[]{:S(2)}) collective-permute-start(bf16[3,256,512]{2,1,0:T(8,128)(2,1)} %all-reduce.7.cloned.1.call-done.mine), channel_id=1, source_target_pairs={{0,1},{1,0},{2,3},{3,2},{4,5},{5,4},{6,7},{7,6},{8,9},{9,8},{10,11... | collective-permute-start | bytes 2359304 | tf_op jit(solution)/shard_map/ppermute | solution.py:96
  121.8 69.6 %collective-permute-start.7 = (bf16[256,256]{1,0:T(8,128)(2,1)S(1)}, bf16[256,256]{1,0:T(8,128)(2,1)S(1)}, u32[]{:S(2)}, u32[]{:S(2)}) collective-permute-start(bf16[256,256]{1,0:T(8,128)(2,1)S(1)} %slice_bitcast_fusion.12), channel_id=1, source_target_pairs={{0,8},{8,16},{16,24},{1,9},{9,17},{17,25},{2,10},{10,18},{18,26},{... | collective-permute-start | bytes 393224 | tf_op jit(solution)/shard_map/ppermute | solution.py:12
  126.1 68.7 %collective-permute-start.3 = (bf16[256,256]{1,0:T(8,128)(2,1)S(1)}, bf16[256,256]{1,0:T(8,128)(2,1)S(1)}, u32[]{:S(2)}, u32[]{:S(2)}) collective-permute-start(bf16[256,256]{1,0:T(8,128)(2,1)S(1)} %slice_bitcast_fusion.13), channel_id=1, source_target_pairs={{0,8},{8,16},{16,24},{1,9},{9,17},{17,25},{2,10},{10,18},{18,26},{... | collective-permute-start | bytes 393224 | tf_op jit(solution)/shard_map/ppermute | solution.py:12
  129.5 110.4 %collective-permute-start.1 = (bf16[3,256,512]{2,1,0:T(8,128)(2,1)}, bf16[3,256,512]{2,1,0:T(8,128)(2,1)}, u32[]{:S(2)}, u32[]{:S(2)}) collective-permute-start(bf16[3,256,512]{2,1,0:T(8,128)(2,1)} %all-reduce.5.cloned.1.call-done.mine), channel_id=1, source_target_pairs={{0,1},{1,0},{2,3},{3,2},{4,5},{5,4},{6,7},{7,6},{8,9},{9,8},{10,11... | collective-permute-start | bytes 2359304 | tf_op jit(solution)/shard_map/ppermute | solution.py:96
  180.5 65.7 %collective-permute-start.6 = (bf16[5,256,512]{2,1,0:T(8,128)(2,1)}, bf16[5,256,512]{2,1,0:T(8,128)(2,1)S(1)}, u32[]{:S(2)}, u32[]{:S(2)}) collective-permute-start(bf16[5,256,512]{2,1,0:T(8,128)(2,1)} %all-reduce.9.cloned.1.call-done.mine), channel_id=1, source_target_pairs={{0,1},{1,0},{2,3},{3,2},{4,5},{5,4},{6,7},{7,6},{8,9},{9,8},{10,11... | collective-permute-start | bytes 3932168 | tf_op jit(solution)/shard_map/ppermute | solution.py:96
  183.9 5.6 %copy-start.10 = (bf16[2048,1024]{1,0:T(8,128)(2,1)S(1)}, bf16[2048,1024]{1,0:T(8,128)(2,1)}, u32[]{:S(2)}) copy-start(bf16[2048,1024]{1,0:T(8,128)(2,1)} %param.3) | copy-start | bytes 12582916
  187.1 55.3 %collective-permute-start.9 = (bf16[256,1024]{1,0:T(8,128)(2,1)}, bf16[256,1024]{1,0:T(8,128)(2,1)}, u32[]{:S(2)}, u32[]{:S(2)}) collective-permute-start(bf16[256,1024]{1,0:T(8,128)(2,1)} %get-tuple-element.14), channel_id=1, source_target_pairs={{8,0},{16,8},{24,16},{9,1},{17,9},{25,17},{10,2},{18,10},{26,18},{... | collective-permute-start | bytes 1572872 | tf_op jit(solution)/shard_map/ppermute | solution.py:12
  191.4 52.8 %collective-permute-start.5 = (bf16[256,1024]{1,0:T(8,128)(2,1)}, bf16[256,1024]{1,0:T(8,128)(2,1)}, u32[]{:S(2)}, u32[]{:S(2)}) collective-permute-start(bf16[256,1024]{1,0:T(8,128)(2,1)} %get-tuple-element.16), channel_id=1, source_target_pairs={{0,8},{8,16},{16,24},{1,9},{9,17},{17,25},{2,10},{10,18},{18,26},{... | collective-permute-start | bytes 1572872 | tf_op jit(solution)/shard_map/ppermute | solution.py:12
  194.8 1.4 collective-permute-start.8
  196.2 1.5 collective-permute-start.4
  239.9 19.9 %collective-permute-start.11 = (bf16[5,256,512]{2,1,0:T(8,128)(2,1)}, bf16[5,256,512]{2,1,0:T(8,128)(2,1)S(1)}, u32[]{:S(2)}, u32[]{:S(2)}) collective-permute-start(bf16[5,256,512]{2,1,0:T(8,128)(2,1)} %all-reduce.11.cloned.1.call-done.mine), channel_id=1, source_target_pairs={{0,1},{1,0},{2,3},{3,2},{4,5},{5,4},{6,7},{7,6},{8,9},{9,8},{10,11... | collective-permute-start | bytes 3932168 | tf_op jit(solution)/shard_map/ppermute | solution.py:96
  244.2 2.0 copy-start.5
  252.8 20.8 %collective-permute-start.10 = (bf16[256,1024]{1,0:T(8,128)(2,1)S(1)}, bf16[256,1024]{1,0:T(8,128)(2,1)S(1)}, u32[]{:S(2)}, u32[]{:S(2)}) collective-permute-start(bf16[256,1024]{1,0:T(8,128)(2,1)S(1)} %get-tuple-element.12), channel_id=1, source_target_pairs={{0,8},{8,16},{16,24},{1,9},{9,17},{17,25},{2,10},{10,18},{18,26},{... | collective-permute-start | bytes 1572872 | tf_op jit(solution)/shard_map/ppermute | solution.py:12
  256.9 2.9 %copy-start.4 = (bf16[5,256,512]{2,1,0:T(8,128)(2,1)S(1)}, bf16[5,256,512]{2,1,0:T(8,128)(2,1)}, u32[]{:S(2)}) copy-start(bf16[5,256,512]{2,1,0:T(8,128)(2,1)} %all-reduce.11.cloned.1.call-done.mine) | copy-start | bytes 3932164
  257.0 16.1 %collective-permute-start.12 = (bf16[256,1024]{1,0:T(8,128)(2,1)S(1)}, bf16[256,1024]{1,0:T(8,128)(2,1)S(1)}, u32[]{:S(2)}, u32[]{:S(2)}) collective-permute-start(bf16[256,1024]{1,0:T(8,128)(2,1)S(1)} %get-tuple-element.10), channel_id=1, source_target_pairs={{8,0},{16,8},{24,16},{9,1},{17,9},{25,17},{10,2},{18,10},{26,18},{... | collective-permute-start | bytes 1572872 | tf_op jit(solution)/shard_map/ppermute | solution.py:12
  274.0 2.3 copy-start.1
  (7 other events, 9.0 us)
Sparse Core Ops, SparseCore 0:
  18.7 50.0 all-reduce.6
  72.1 48.7 all-reduce.4
  123.9 56.4 all-reduce.8
  183.4 56.4 all-reduce.10
